TPU v7x, 32 devices: a whole 2x2x4 slice. The times are simulated.
32 devices in a mesh: gx: 4 (over z), gy: 2 (over y), gz: 4 (over x, core).
Axes of the slice: x: 2, y: 2, z: 4, core: 2. Of those that a mesh axis runs over, the one named last changes fastest.
Arguments:
- adjoint_fields: float32 [6, 1, 16, 16, 512], P(None, None, 'gx', 'gy', 'gz'), may hold values from -6 to 6
- forward_fields: bfloat16 [2, 3, 1, 16, 16, 512], P(None, None, None, 'gx', 'gy', 'gz'), may hold values from -6 to 6
- rock_unit: int32 [16, 16, 512], P('gx', 'gy', 'gz'), may hold values from 0 to 31
- unit_conductivity: int32 [32], replicated, may hold values from 50 to 2000
- receiver_cells: int32 [256], replicated, may hold values from 0 to 131071
- residuals: float32 [2, 1, 256], replicated, may hold values from -6 to 6
- model_vectors: float32 [16, 4, 16, 512], P('gx', None, 'gy', 'gz'), may hold values from -6 to 6
Outputs:
- adjoint_state: float32 [6, 1, 16, 16, 512], P(None, None, 'gx', 'gy', 'gz')
- normal_product: float32 [16, 4, 16, 512], P('gx', None, 'gy', 'gz')
Inputs may be any that keep to these rules, and one draw needn't show every extreme that they name: `rock_unit`: each entry is a rock unit number. `receiver_cells`: a receiver's linear cell index; two receivers may share a cell.
All inputs are finite; a program needn't handle non-finite values.
Results may differ from a plain program's by a relative error of at most 0.00075.
Values sent between devices are 32-bit elements; how exact they have to be, the bound alone decides.
A program may use at most 64 MiB of HBM per device.

v0:
```python
import math
import jax
import jax.numpy as jnp
from jax import lax
from jax.sharding import PartitionSpec as P

LOSS_FACTOR = 0.5
COURANT = 0.5


def padded_2(block, sides, width):
    for axis, dim in sides:
        count = lax.axis_size(axis)
        forward = [(i, i + 1) for i in range(count - 1)]
        backward = [(target, source) for source, target in forward]
        low = lax.ppermute(
            lax.slice_in_dim(block, block.shape[dim] - width, None, axis=dim), axis, forward
        )
        high = lax.ppermute(lax.slice_in_dim(block, 0, width, axis=dim), axis, backward)
        block = jnp.concatenate([low, block, high], axis=dim)
    return block


def crop(array, outer, inner):
    cut = outer - inner
    if cut == 0:
        return array
    return array[..., cut:-cut, cut:-cut, cut:-cut]


def local(
    adjoint_fields,
    forward_fields,
    rock_unit,
    unit_conductivity,
    receiver_cells,
    residuals,
    model_vectors,
):
    moments = forward_fields.shape[0]
    sources = adjoint_fields.shape[1]
    tile_x, tile_y, tile_z = rock_unit.shape
    whole_x = tile_x * lax.axis_size("gx")
    whole_y = tile_y * lax.axis_size("gy")
    whole_z = tile_z * lax.axis_size("gz")
    unit_count = unit_conductivity.shape[0]
    labels = lax.broadcasted_iota(jnp.int32, (unit_count, 1, 1, 1), 0)
    looked_up = jnp.sum(
        jnp.where(rock_unit[None] == labels, unit_conductivity[:, None, None, None], 0), axis=0
    )
    conductivity = looked_up.astype(jnp.float32) * 0.001
    depth = 1
    damping = LOSS_FACTOR * conductivity
    keep_ext = (1.0 - damping) / (1.0 + damping)
    drive_ext = COURANT / (1.0 + damping)
    sigma_tile = crop(conductivity, depth - 1, 0)
    anchor_x = lax.axis_index("gx") * tile_x
    anchor_y = lax.axis_index("gy") * tile_y
    anchor_z = lax.axis_index("gz") * tile_z
    coord_x = lax.broadcasted_iota(jnp.int32, (tile_x + 2 * depth, 1, 1), 0) + anchor_x - depth
    coord_y = lax.broadcasted_iota(jnp.int32, (1, tile_y + 2 * depth, 1), 1) + anchor_y - depth
    coord_z = lax.broadcasted_iota(jnp.int32, (1, 1, tile_z + 2 * depth), 2) + anchor_z - depth
    inside = (
        (coord_x >= 0)
        & (coord_x < whole_x)
        & (coord_y >= 0)
        & (coord_y < whole_y)
        & (coord_z >= 0)
        & (coord_z < whole_z)
    )
    margin = depth - 1
    ext_x = tile_x + 2 * margin
    ext_y = tile_y + 2 * margin
    ext_z = tile_z + 2 * margin
    local_x = receiver_cells // (whole_y * whole_z) - anchor_x + margin
    local_y = receiver_cells // whole_z % whole_y - anchor_y + margin
    local_z = receiver_cells % whole_z - anchor_z + margin
    within = (
        (local_x >= 0)
        & (local_x < ext_x)
        & (local_y >= 0)
        & (local_y < ext_y)
        & (local_z >= 0)
        & (local_z < ext_z)
    )
    ext_cells = ext_x * ext_y * ext_z
    flat_index = jnp.where(within, (local_x * ext_y + local_y) * ext_z + local_z, ext_cells)
    state = adjoint_fields
    panels = []
    for block in range(moments // depth):
        padded = padded_2(state, (("gx", 2), ("gy", 3), ("gz", 4)), 1)
        moment = block * depth
        electric = padded[0:3]
        magnetic = padded[3:6]
        tile_e = crop(electric, depth, 0)
        forward_f = forward_fields[moment].astype(jnp.float32)
        panels.append(
            sigma_tile
            * (forward_f[0] * tile_e[0] + forward_f[1] * tile_e[1] + forward_f[2] * tile_e[2])
        )
        electric_base = electric[:, :, :-1, :-1, :-1]
        magnetic_base = magnetic[:, :, :-1, :-1, :-1]
        along_x = electric[:, :, 1:, :-1, :-1] - electric_base
        along_y = electric[:, :, :-1, 1:, :-1] - electric_base
        along_z = electric[:, :, :-1, :-1, 1:] - electric_base
        new_h = jnp.stack(
            [
                magnetic_base[0] - COURANT * (along_y[2] - along_z[1]),
                magnetic_base[1] - COURANT * (along_z[0] - along_x[2]),
                magnetic_base[2] - COURANT * (along_x[1] - along_y[0]),
            ]
        )
        h_mask = crop(inside, depth, depth)[:-1, :-1, :-1]
        new_h = jnp.where(h_mask, new_h, 0.0)
        inner_h = new_h[:, :, 1:, 1:, 1:]
        back_x = inner_h - new_h[:, :, :-1, 1:, 1:]
        back_y = inner_h - new_h[:, :, 1:, :-1, 1:]
        back_z = inner_h - new_h[:, :, 1:, 1:, :-1]
        inject_ext = (
            jnp.zeros((sources, ext_cells), jnp.float32)
            .at[:, flat_index]
            .add(residuals[moment], mode="drop")
        )
        inject_ext = inject_ext.reshape(sources, ext_x, ext_y, ext_z)
        inject = crop(inject_ext, margin, depth - 1)
        keep_rate = crop(keep_ext, margin, depth - 1)
        drive_rate = crop(drive_ext, margin, depth - 1)
        middle_e = electric[:, :, 1:-1, 1:-1, 1:-1]
        new_e = jnp.stack(
            [
                keep_rate * middle_e[0] + drive_rate * (back_y[2] - back_z[1] + inject),
                keep_rate * middle_e[1] + drive_rate * (back_z[0] - back_x[2]),
                keep_rate * middle_e[2] + drive_rate * (back_x[1] - back_y[0]),
            ]
        )
        new_e = jnp.where(crop(inside, depth, depth - 1), new_e, 0.0)
        padded = jnp.concatenate([new_e, inner_h], axis=0)
        state = padded
    panel_rows = jnp.stack(panels).reshape(moments * sources, tile_x, tile_y, tile_z)
    scale_factor = 1.0 / math.sqrt(float(moments * sources) * float(whole_x * whole_y * whole_z))
    local_w = jnp.einsum(
        "kxyz,xnyz->kn", panel_rows, model_vectors, precision=lax.Precision.HIGHEST
    )
    weights = lax.psum(local_w, ("gx", "gy", "gz"))
    normal_product = scale_factor * jnp.einsum(
        "kxyz,kn->xnyz", panel_rows, weights, precision=lax.Precision.HIGHEST
    )
    return (state, normal_product)


def solution(mesh):
    in_specs = (
        P(None, None, "gx", "gy", "gz"),
        P(None, None, None, "gx", "gy", "gz"),
        P("gx", "gy", "gz"),
        P(),
        P(),
        P(),
        P("gx", None, "gy", "gz"),
    )
    out_specs = (P(None, None, "gx", "gy", "gz"), P("gx", None, "gy", "gz"))
    return jax.shard_map(local, mesh=mesh, in_specs=in_specs, out_specs=out_specs, check_vma=False)
```

profile of v0, /device:TPU:0, one launch (start us, length us, event | category | flops | bytes accessed | tf_op | source)
XLA Modules:
  0.0 104.1 jit_solution(2446326424200641260)
XLA Ops:
  0.7 0.8 fusion.61
  1.5 4.9 %collective-permute-start = (f32[6,1,1,8,128]{4,3,2,1,0:T(8,128)S(1)}, f32[6,1,1,8,128]{4,3,2,1,0:T(8,128)S(1)}, u32[]{:S(2)}, u32[]{:S(2)}) collective-permute-start(f32[6,1,1,8,128]{4,3,2,1,0:T(8,128)S(1)} %get-tuple-element.45), channel_id=1, source_target_pairs={{0,8},{8,16},{16,24},{1,9},{9,17},{17,25},{2,10},{10,18},{18,26},{... | collective-permute-start | bytes 73736 | tf_op jit(solution)/shard_map/ppermute | solution.py:16
  6.4 1.3 %collective-permute-start.1 = (f32[6,1,1,8,128]{4,3,2,1,0:T(8,128)S(1)}, f32[6,1,1,8,128]{4,3,2,1,0:T(8,128)S(1)}, u32[]{:S(2)}, u32[]{:S(2)}) collective-permute-start(f32[6,1,1,8,128]{4,3,2,1,0:T(8,128)S(1)} %get-tuple-element.44), channel_id=1, source_target_pairs={{8,0},{16,8},{24,16},{9,1},{17,9},{25,17},{10,2},{18,10},{26,18},{... | collective-permute-start | bytes 73736 | tf_op jit(solution)/shard_map/ppermute | solution.py:19
  7.9 0.6 copy-done.4
  8.7 3.4 %collective-permute-done.1 = f32[6,1,1,8,128]{4,3,2,1,0:T(8,128)S(1)} collective-permute-done((f32[6,1,1,8,128]{4,3,2,1,0:T(8,128)S(1)}, f32[6,1,1,8,128]{4,3,2,1,0:T(8,128)S(1)}, u32[]{:S(2)}, u32[]{:S(2)}) %collective-permute-start.1) | collective-permute-done | bytes 24608 | tf_op jit(solution)/shard_map/ppermute | solution.py:19
  12.1 3.4 %collective-permute-start.2 = (f32[6,1,6,1,128]{4,3,2,1,0:T(1,128)S(1)}, f32[6,1,6,1,128]{4,3,2,1,0:T(1,128)S(1)}, u32[]{:S(2)}, u32[]{:S(2)}) collective-permute-start(f32[6,1,6,1,128]{4,3,2,1,0:T(1,128)S(1)} %get-tuple-element.36), channel_id=1, source_target_pairs={{0,4},{1,5},{2,6},{3,7},{8,12},{9,13},{10,14},{11,15},{16,20},{17,... | collective-permute-start | bytes 55304 | tf_op jit(solution)/shard_map/ppermute | solution.py:16
  15.6 1.3 %collective-permute-start.3 = (f32[6,1,6,1,128]{4,3,2,1,0:T(1,128)S(1)}, f32[6,1,6,1,128]{4,3,2,1,0:T(1,128)S(1)}, u32[]{:S(2)}, u32[]{:S(2)}) collective-permute-start(f32[6,1,6,1,128]{4,3,2,1,0:T(1,128)S(1)} %get-tuple-element.37), channel_id=1, source_target_pairs={{4,0},{5,1},{6,2},{7,3},{12,8},{13,9},{14,10},{15,11},{20,16},{21,... | collective-permute-start | bytes 55304 | tf_op jit(solution)/shard_map/ppermute | solution.py:19
  17.0 4.2 %collective-permute-done.3 = f32[6,1,6,1,128]{4,3,2,1,0:T(1,128)S(1)} collective-permute-done((f32[6,1,6,1,128]{4,3,2,1,0:T(1,128)S(1)}, f32[6,1,6,1,128]{4,3,2,1,0:T(1,128)S(1)}, u32[]{:S(2)}, u32[]{:S(2)}) %collective-permute-start.3) | collective-permute-done | bytes 18464 | tf_op jit(solution)/shard_map/ppermute | solution.py:19
  21.5 1.3 %collective-permute-start.4 = (f32[6,1,6,10,1]{4,3,2,1,0:T(8,128)S(1)}, f32[6,1,6,10,1]{4,3,2,1,0:T(8,128)S(1)}, u32[]{:S(2)}, u32[]{:S(2)}) collective-permute-start(f32[6,1,6,10,1]{4,3,2,1,0:T(8,128)S(1)} %get-tuple-element.22), channel_id=1, source_target_pairs={{0,1},{1,2},{2,3},{4,5},{5,6},{6,7},{8,9},{9,10},{10,11},{12,13},{... | collective-permute-start | bytes 4328 | tf_op jit(solution)/shard_map/ppermute | solution.py:16
  23.0 1.9 %scatter_custom_fusion = f32[4096]{0:T(1024)S(1)} fusion(s32[256]{0:T(256)S(1)} %compare_select_fusion, f32[256]{0:T(256)S(1)} %bitcast.93, f32[]{:T(128)} %constant.92.clone.1), kind=kCustom, calls=%fused_computation.122 | custom fusion | flops 256 | bytes 16388 | tf_op jit(solution)/shard_map/scatter-add | solution.py:122
  25.0 1.3 %collective-permute-start.5 = (f32[6,1,6,10,1]{4,3,2,1,0:T(8,128)S(1)}, f32[6,1,6,10,1]{4,3,2,1,0:T(8,128)S(1)}, u32[]{:S(2)}, u32[]{:S(2)}) collective-permute-start(f32[6,1,6,10,1]{4,3,2,1,0:T(8,128)S(1)} %get-tuple-element.21), channel_id=1, source_target_pairs={{1,0},{2,1},{3,2},{5,4},{6,5},{7,6},{9,8},{10,9},{11,10},{13,12},{... | collective-permute-start | bytes 4328 | tf_op jit(solution)/shard_map/ppermute | solution.py:19
  26.3 0.4 maximum_maximum_fusion
  26.6 3.5 %collective-permute-done.5 = f32[6,1,6,10,1]{4,3,2,1,0:T(8,128)S(1)} collective-permute-done((f32[6,1,6,10,1]{4,3,2,1,0:T(8,128)S(1)}, f32[6,1,6,10,1]{4,3,2,1,0:T(8,128)S(1)}, u32[]{:S(2)}, u32[]{:S(2)}) %collective-permute-start.5) | collective-permute-done | bytes 1472 | tf_op jit(solution)/shard_map/ppermute | solution.py:19
  30.2 0.2 fusion.14
  30.7 3.5 %collective-permute-start.6 = (f32[6,1,1,8,128]{4,3,2,1,0:T(8,128)S(1)}, f32[6,1,1,8,128]{4,3,2,1,0:T(8,128)S(1)}, u32[]{:S(2)}, u32[]{:S(2)}) collective-permute-start(f32[6,1,1,8,128]{4,3,2,1,0:T(8,128)S(1)} %get-tuple-element.42), channel_id=1, source_target_pairs={{0,8},{8,16},{16,24},{1,9},{9,17},{17,25},{2,10},{10,18},{18,26},{... | collective-permute-start | bytes 73736 | tf_op jit(solution)/shard_map/ppermute | solution.py:16
  34.2 1.3 %collective-permute-start.7 = (f32[6,1,1,8,128]{4,3,2,1,0:T(8,128)S(1)}, f32[6,1,1,8,128]{4,3,2,1,0:T(8,128)S(1)}, u32[]{:S(2)}, u32[]{:S(2)}) collective-permute-start(f32[6,1,1,8,128]{4,3,2,1,0:T(8,128)S(1)} %get-tuple-element.43), channel_id=1, source_target_pairs={{8,0},{16,8},{24,16},{9,1},{17,9},{25,17},{10,2},{18,10},{26,18},{... | collective-permute-start | bytes 73736 | tf_op jit(solution)/shard_map/ppermute | solution.py:19
  35.5 0.2 collective-permute-done.6
  35.7 4.2 %collective-permute-done.7 = f32[6,1,1,8,128]{4,3,2,1,0:T(8,128)S(1)} collective-permute-done((f32[6,1,1,8,128]{4,3,2,1,0:T(8,128)S(1)}, f32[6,1,1,8,128]{4,3,2,1,0:T(8,128)S(1)}, u32[]{:S(2)}, u32[]{:S(2)}) %collective-permute-start.7) | collective-permute-done | bytes 24608 | tf_op jit(solution)/shard_map/ppermute | solution.py:19
  39.9 1.6 %collective-permute-start.8 = (f32[6,1,6,1,128]{4,3,2,1,0:T(1,128)S(1)}, f32[6,1,6,1,128]{4,3,2,1,0:T(1,128)S(1)}, u32[]{:S(2)}, u32[]{:S(2)}) collective-permute-start(f32[6,1,6,1,128]{4,3,2,1,0:T(1,128)S(1)} %get-tuple-element.34), channel_id=1, source_target_pairs={{0,4},{1,5},{2,6},{3,7},{8,12},{9,13},{10,14},{11,15},{16,20},{17,... | collective-permute-start | bytes 55304 | tf_op jit(solution)/shard_map/ppermute | solution.py:16
  41.6 1.3 %collective-permute-start.9 = (f32[6,1,6,1,128]{4,3,2,1,0:T(1,128)S(1)}, f32[6,1,6,1,128]{4,3,2,1,0:T(1,128)S(1)}, u32[]{:S(2)}, u32[]{:S(2)}) collective-permute-start(f32[6,1,6,1,128]{4,3,2,1,0:T(1,128)S(1)} %get-tuple-element.35), channel_id=1, source_target_pairs={{4,0},{5,1},{6,2},{7,3},{12,8},{13,9},{14,10},{15,11},{20,16},{21,... | collective-permute-start | bytes 55304 | tf_op jit(solution)/shard_map/ppermute | solution.py:19
  43.0 4.2 %collective-permute-done.9 = f32[6,1,6,1,128]{4,3,2,1,0:T(1,128)S(1)} collective-permute-done((f32[6,1,6,1,128]{4,3,2,1,0:T(1,128)S(1)}, f32[6,1,6,1,128]{4,3,2,1,0:T(1,128)S(1)}, u32[]{:S(2)}, u32[]{:S(2)}) %collective-permute-start.9) | collective-permute-done | bytes 18464 | tf_op jit(solution)/shard_map/ppermute | solution.py:19
  47.4 4.1 %collective-permute-start.10 = (f32[6,1,6,10,1]{4,3,2,1,0:T(8,128)S(1)}, f32[6,1,6,10,1]{4,3,2,1,0:T(8,128)S(1)}, u32[]{:S(2)}, u32[]{:S(2)}) collective-permute-start(f32[6,1,6,10,1]{4,3,2,1,0:T(8,128)S(1)} %get-tuple-element.20), channel_id=1, source_target_pairs={{0,1},{1,2},{2,3},{4,5},{5,6},{6,7},{8,9},{9,10},{10,11},{12,13},{... | collective-permute-start | bytes 4328 | tf_op jit(solution)/shard_map/ppermute | solution.py:16
  51.6 1.9 %scatter_custom_fusion.1 = f32[4096]{0:T(1024)S(1)} fusion(s32[256]{0:T(256)S(1)} %compare_select_fusion, f32[256]{0:T(256)S(1)} %bitcast.92, f32[]{:T(128)} %constant.92.clone.1), kind=kCustom, calls=%fused_computation.120 | custom fusion | flops 256 | bytes 16388 | tf_op jit(solution)/shard_map/scatter-add | solution.py:122
  53.5 1.3 %collective-permute-start.11 = (f32[6,1,6,10,1]{4,3,2,1,0:T(8,128)S(1)}, f32[6,1,6,10,1]{4,3,2,1,0:T(8,128)S(1)}, u32[]{:S(2)}, u32[]{:S(2)}) collective-permute-start(f32[6,1,6,10,1]{4,3,2,1,0:T(8,128)S(1)} %get-tuple-element.19), channel_id=1, source_target_pairs={{1,0},{2,1},{3,2},{5,4},{6,5},{7,6},{9,8},{10,9},{11,10},{13,12},{... | collective-permute-start | bytes 4328 | tf_op jit(solution)/shard_map/ppermute | solution.py:19
  54.8 0.4 maximum_maximum_fusion.1
  55.2 4.0 %collective-permute-done.11 = f32[6,1,6,10,1]{4,3,2,1,0:T(8,128)S(1)} collective-permute-done((f32[6,1,6,10,1]{4,3,2,1,0:T(8,128)S(1)}, f32[6,1,6,10,1]{4,3,2,1,0:T(8,128)S(1)}, u32[]{:S(2)}, u32[]{:S(2)}) %collective-permute-start.11) | collective-permute-done | bytes 1472 | tf_op jit(solution)/shard_map/ppermute | solution.py:19
  59.4 0.2 fusion.8
  59.8 0.4 convolution_bitcast_fusion
  60.1 42.4 %psum.7 = f32[2,4]{1,0:T(2,128)S(1)} all-reduce(f32[2,4]{1,0:T(2,128)S(1)} %convolution_bitcast_fusion), channel_id=1, replica_groups=mesh['gx'=4,'gy'=2,'gz'=4] {'gx','gy','gz'}, use_global_device_ids=true, to_apply=%region_3.4 | all-reduce | flops 8 | bytes 64 | tf_op jit(solution)/shard_map/psum | solution.py:144
  102.5 0.3 fusion
  102.8 0.6 copy.56
  103.5 0.6 pad_maximum_fusion.11
  (51 shorter events, 1.9 us)
Async XLA Ops:
  0.6 59.1 %copy-start = (f32[4,4,8,128]{3,2,1,0:T(8,128)S(1)}, f32[4,4,8,128]{3,2,1,0:T(8,128)}, u32[]{:S(2)}) copy-start(f32[4,4,8,128]{3,2,1,0:T(8,128)} %param.13) | copy-start | bytes 196612
  0.6 7.1 %copy-start.2 = (bf16[2,3,1,4,8,128]{5,4,3,2,1,0:T(8,128)(2,1)S(1)}, bf16[2,3,1,4,8,128]{5,4,3,2,1,0:T(8,128)(2,1)}, u32[]{:S(2)}) copy-start(bf16[2,3,1,4,8,128]{5,4,3,2,1,0:T(8,128)(2,1)} %param.8) | copy-start | bytes 147460
  1.5 7.1 %collective-permute-start = (f32[6,1,1,8,128]{4,3,2,1,0:T(8,128)S(1)}, f32[6,1,1,8,128]{4,3,2,1,0:T(8,128)S(1)}, u32[]{:S(2)}, u32[]{:S(2)}) collective-permute-start(f32[6,1,1,8,128]{4,3,2,1,0:T(8,128)S(1)} %get-tuple-element.45), channel_id=1, source_target_pairs={{0,8},{8,16},{16,24},{1,9},{9,17},{17,25},{2,10},{10,18},{18,26},{... | collective-permute-start | bytes 73736 | tf_op jit(solution)/shard_map/ppermute | solution.py:16
  6.4 5.7 %collective-permute-start.1 = (f32[6,1,1,8,128]{4,3,2,1,0:T(8,128)S(1)}, f32[6,1,1,8,128]{4,3,2,1,0:T(8,128)S(1)}, u32[]{:S(2)}, u32[]{:S(2)}) collective-permute-start(f32[6,1,1,8,128]{4,3,2,1,0:T(8,128)S(1)} %get-tuple-element.44), channel_id=1, source_target_pairs={{8,0},{16,8},{24,16},{9,1},{17,9},{25,17},{10,2},{18,10},{26,18},{... | collective-permute-start | bytes 73736 | tf_op jit(solution)/shard_map/ppermute | solution.py:19
  7.7 0.9 copy-start.1
  7.9 0.7 copy-start.4
  12.1 4.7 %copy-start.5 = (s32[256]{0:T(256)S(1)}, s32[256]{0:T(256)}, u32[]{:S(2)}) copy-start(s32[256]{0:T(256)} %param.11) | copy-start | bytes 3076
  12.1 4.9 %collective-permute-start.2 = (f32[6,1,6,1,128]{4,3,2,1,0:T(1,128)S(1)}, f32[6,1,6,1,128]{4,3,2,1,0:T(1,128)S(1)}, u32[]{:S(2)}, u32[]{:S(2)}) collective-permute-start(f32[6,1,6,1,128]{4,3,2,1,0:T(1,128)S(1)} %get-tuple-element.36), channel_id=1, source_target_pairs={{0,4},{1,5},{2,6},{3,7},{8,12},{9,13},{10,14},{11,15},{16,20},{17,... | collective-permute-start | bytes 55304 | tf_op jit(solution)/shard_map/ppermute | solution.py:16
  15.6 5.7 %collective-permute-start.3 = (f32[6,1,6,1,128]{4,3,2,1,0:T(1,128)S(1)}, f32[6,1,6,1,128]{4,3,2,1,0:T(1,128)S(1)}, u32[]{:S(2)}, u32[]{:S(2)}) collective-permute-start(f32[6,1,6,1,128]{4,3,2,1,0:T(1,128)S(1)} %get-tuple-element.37), channel_id=1, source_target_pairs={{4,0},{5,1},{6,2},{7,3},{12,8},{13,9},{14,10},{15,11},{20,16},{21,... | collective-permute-start | bytes 55304 | tf_op jit(solution)/shard_map/ppermute | solution.py:19
  21.3 1.5 %copy-start.3 = (s32[4,8,128]{2,1,0:T(8,128)S(1)}, s32[4,8,128]{2,1,0:T(8,128)}, u32[]{:S(2)}) copy-start(s32[4,8,128]{2,1,0:T(8,128)} %param.9) | copy-start | bytes 49156
  21.5 1.3 %copy-start.6 = (s32[32]{0:T(128)S(1)}, s32[32]{0:T(128)}, u32[]{:S(2)}) copy-start(s32[32]{0:T(128)} %param.10) | copy-start | bytes 388
  21.5 4.8 %collective-permute-start.4 = (f32[6,1,6,10,1]{4,3,2,1,0:T(8,128)S(1)}, f32[6,1,6,10,1]{4,3,2,1,0:T(8,128)S(1)}, u32[]{:S(2)}, u32[]{:S(2)}) collective-permute-start(f32[6,1,6,10,1]{4,3,2,1,0:T(8,128)S(1)} %get-tuple-element.22), channel_id=1, source_target_pairs={{0,1},{1,2},{2,3},{4,5},{5,6},{6,7},{8,9},{9,10},{10,11},{12,13},{... | collective-permute-start | bytes 4328 | tf_op jit(solution)/shard_map/ppermute | solution.py:16
  25.0 5.2 %collective-permute-start.5 = (f32[6,1,6,10,1]{4,3,2,1,0:T(8,128)S(1)}, f32[6,1,6,10,1]{4,3,2,1,0:T(8,128)S(1)}, u32[]{:S(2)}, u32[]{:S(2)}) collective-permute-start(f32[6,1,6,10,1]{4,3,2,1,0:T(8,128)S(1)} %get-tuple-element.21), channel_id=1, source_target_pairs={{1,0},{2,1},{3,2},{5,4},{6,5},{7,6},{9,8},{10,9},{11,10},{13,12},{... | collective-permute-start | bytes 4328 | tf_op jit(solution)/shard_map/ppermute | solution.py:19
  30.7 5.0 %collective-permute-start.6 = (f32[6,1,1,8,128]{4,3,2,1,0:T(8,128)S(1)}, f32[6,1,1,8,128]{4,3,2,1,0:T(8,128)S(1)}, u32[]{:S(2)}, u32[]{:S(2)}) collective-permute-start(f32[6,1,1,8,128]{4,3,2,1,0:T(8,128)S(1)} %get-tuple-element.42), channel_id=1, source_target_pairs={{0,8},{8,16},{16,24},{1,9},{9,17},{17,25},{2,10},{10,18},{18,26},{... | collective-permute-start | bytes 73736 | tf_op jit(solution)/shard_map/ppermute | solution.py:16
  34.2 5.7 %collective-permute-start.7 = (f32[6,1,1,8,128]{4,3,2,1,0:T(8,128)S(1)}, f32[6,1,1,8,128]{4,3,2,1,0:T(8,128)S(1)}, u32[]{:S(2)}, u32[]{:S(2)}) collective-permute-start(f32[6,1,1,8,128]{4,3,2,1,0:T(8,128)S(1)} %get-tuple-element.43), channel_id=1, source_target_pairs={{8,0},{16,8},{24,16},{9,1},{17,9},{25,17},{10,2},{18,10},{26,18},{... | collective-permute-start | bytes 73736 | tf_op jit(solution)/shard_map/ppermute | solution.py:19
  39.9 3.1 %collective-permute-start.8 = (f32[6,1,6,1,128]{4,3,2,1,0:T(1,128)S(1)}, f32[6,1,6,1,128]{4,3,2,1,0:T(1,128)S(1)}, u32[]{:S(2)}, u32[]{:S(2)}) collective-permute-start(f32[6,1,6,1,128]{4,3,2,1,0:T(1,128)S(1)} %get-tuple-element.34), channel_id=1, source_target_pairs={{0,4},{1,5},{2,6},{3,7},{8,12},{9,13},{10,14},{11,15},{16,20},{17,... | collective-permute-start | bytes 55304 | tf_op jit(solution)/shard_map/ppermute | solution.py:16
  41.6 5.7 %collective-permute-start.9 = (f32[6,1,6,1,128]{4,3,2,1,0:T(1,128)S(1)}, f32[6,1,6,1,128]{4,3,2,1,0:T(1,128)S(1)}, u32[]{:S(2)}, u32[]{:S(2)}) collective-permute-start(f32[6,1,6,1,128]{4,3,2,1,0:T(1,128)S(1)} %get-tuple-element.35), channel_id=1, source_target_pairs={{4,0},{5,1},{6,2},{7,3},{12,8},{13,9},{14,10},{15,11},{20,16},{21,... | collective-permute-start | bytes 55304 | tf_op jit(solution)/shard_map/ppermute | solution.py:19
  47.4 7.4 %collective-permute-start.10 = (f32[6,1,6,10,1]{4,3,2,1,0:T(8,128)S(1)}, f32[6,1,6,10,1]{4,3,2,1,0:T(8,128)S(1)}, u32[]{:S(2)}, u32[]{:S(2)}) collective-permute-start(f32[6,1,6,10,1]{4,3,2,1,0:T(8,128)S(1)} %get-tuple-element.20), channel_id=1, source_target_pairs={{0,1},{1,2},{2,3},{4,5},{5,6},{6,7},{8,9},{9,10},{10,11},{12,13},{... | collective-permute-start | bytes 4328 | tf_op jit(solution)/shard_map/ppermute | solution.py:16
  53.5 5.7 %collective-permute-start.11 = (f32[6,1,6,10,1]{4,3,2,1,0:T(8,128)S(1)}, f32[6,1,6,10,1]{4,3,2,1,0:T(8,128)S(1)}, u32[]{:S(2)}, u32[]{:S(2)}) collective-permute-start(f32[6,1,6,10,1]{4,3,2,1,0:T(8,128)S(1)} %get-tuple-element.19), channel_id=1, source_target_pairs={{1,0},{2,1},{3,2},{5,4},{6,5},{7,6},{9,8},{10,9},{11,10},{13,12},{... | collective-permute-start | bytes 4328 | tf_op jit(solution)/shard_map/ppermute | solution.py:19
where the time goes:
time: 105 us; the launch traced here: 104 us
  blocking collectives  42.4 us (40%)
  starting transfers between devices  26.6 us (25%)
  waiting for transfers between devices  24 us (23%)
  other arithmetic  6.79 us (6%)
  local copies, waits for them, and re-layouts  2.56 us (2%)
  between operations  1.06 us (1%)
    psum x1, blocking collectives, local(): weights = lax.psum(local_w, ('gx', 'gy', 'gz'))  42.4 us
    ppermute x6, waiting for transfers between devices, padded_2(): lax.ppermute(lax.slice_in_dim(block, 0, width, axis=dim), axis, backward)  23.6 us
    ppermute x6, starting transfers between devices, padded_2(): lax.ppermute(lax.slice_in_dim(block, block.shape[dim] - width, None, axis...  18.9 us
    ppermute x6, starting transfers between devices, padded_2(): lax.ppermute(lax.slice_in_dim(block, 0, width, axis=dim), axis, backward)  7.75 us
    scatter-add x2, other arithmetic, local(): inject_ext = jnp.zeros((sources, ext_cells), jnp.float32).at[:, flat_inde...  3.88 us
  transfers between devices with their start and end apart: 12, of which 9 were waited for; matrix products, arithmetic and copies ran while one was open for 5% of the time, Pallas kernels for 0%

commit v1 on v0

--- a/solution.py
+++ b/solution.py
@@ -141,7 +141,8 @@
     local_w = jnp.einsum(
         "kxyz,xnyz->kn", panel_rows, model_vectors, precision=lax.Precision.HIGHEST
     )
-    weights = lax.psum(local_w, ("gx", "gy", "gz"))
+    half = lax.psum(local_w, ("gy", "gz"))
+    weights = lax.psum(half, "gx")
     normal_product = scale_factor * jnp.einsum(
         "kxyz,kn->xnyz", panel_rows, weights, precision=lax.Precision.HIGHEST
     )

time: 105 us -> 89.1 us (0.85)
  blocking collectives: 42.4 us -> 26.8 us
    psum x1 -> x2, blocking collectives: 42.4 us -> 26.8 us  [the longest x1 16.9 us: local(): half = lax.psum(local_w, ('gy', 'gz'))]
  transfers between devices with their start and end apart: 12 -> 12, of which waited for: 9 -> 9; matrix products, arithmetic and copies ran while one was open for 5% -> 6% of each run, Pallas kernels for 0% -> 0%
where the time goes in v1:
time: 89.1 us; the launch traced here: 88.6 us
  blocking collectives  26.8 us (30%)
  starting transfers between devices  26.6 us (30%)
  waiting for transfers between devices  24 us (27%)
  other arithmetic  6.79 us (8%)
  local copies, waits for them, and re-layouts  2.56 us (3%)
  between operations  1.06 us (1%)
    ppermute x6, waiting for transfers between devices, padded_2(): lax.ppermute(lax.slice_in_dim(block, 0, width, axis=dim), axis, backward)  23.6 us
    ppermute x6, starting transfers between devices, padded_2(): lax.ppermute(lax.slice_in_dim(block, block.shape[dim] - width, None, axis...  18.9 us
    psum x1, blocking collectives, local(): half = lax.psum(local_w, ('gy', 'gz'))  16.9 us
    psum x1, blocking collectives, local(): weights = lax.psum(half, 'gx')  9.93 us
    ppermute x6, starting transfers between devices, padded_2(): lax.ppermute(lax.slice_in_dim(block, 0, width, axis=dim), axis, backward)  7.75 us
    scatter-add x2, other arithmetic, local(): inject_ext = jnp.zeros((sources, ext_cells), jnp.float32).at[:, flat_inde...  3.88 us
  transfers between devices with their start and end apart: 12, of which 9 were waited for; matrix products, arithmetic and copies ran while one was open for 6% of the time, Pallas kernels for 0%

profile of v1, /device:TPU:0, one launch (start us, length us, event | category | flops | bytes accessed | tf_op | source)
XLA Modules:
  0.0 88.6 jit_solution(313875202802181757)
XLA Ops:
  0.7 0.8 fusion.61
  1.5 4.9 %collective-permute-start = (f32[6,1,1,8,128]{4,3,2,1,0:T(8,128)S(1)}, f32[6,1,1,8,128]{4,3,2,1,0:T(8,128)S(1)}, u32[]{:S(2)}, u32[]{:S(2)}) collective-permute-start(f32[6,1,1,8,128]{4,3,2,1,0:T(8,128)S(1)} %get-tuple-element.45), channel_id=1, source_target_pairs={{0,8},{8,16},{16,24},{1,9},{9,17},{17,25},{2,10},{10,18},{18,26},{... | collective-permute-start | bytes 73736 | tf_op jit(solution)/shard_map/ppermute | solution.py:16
  6.4 1.3 %collective-permute-start.1 = (f32[6,1,1,8,128]{4,3,2,1,0:T(8,128)S(1)}, f32[6,1,1,8,128]{4,3,2,1,0:T(8,128)S(1)}, u32[]{:S(2)}, u32[]{:S(2)}) collective-permute-start(f32[6,1,1,8,128]{4,3,2,1,0:T(8,128)S(1)} %get-tuple-element.44), channel_id=1, source_target_pairs={{8,0},{16,8},{24,16},{9,1},{17,9},{25,17},{10,2},{18,10},{26,18},{... | collective-permute-start | bytes 73736 | tf_op jit(solution)/shard_map/ppermute | solution.py:19
  7.9 0.6 copy-done.4
  8.7 3.4 %collective-permute-done.1 = f32[6,1,1,8,128]{4,3,2,1,0:T(8,128)S(1)} collective-permute-done((f32[6,1,1,8,128]{4,3,2,1,0:T(8,128)S(1)}, f32[6,1,1,8,128]{4,3,2,1,0:T(8,128)S(1)}, u32[]{:S(2)}, u32[]{:S(2)}) %collective-permute-start.1) | collective-permute-done | bytes 24608 | tf_op jit(solution)/shard_map/ppermute | solution.py:19
  12.1 3.4 %collective-permute-start.2 = (f32[6,1,6,1,128]{4,3,2,1,0:T(1,128)S(1)}, f32[6,1,6,1,128]{4,3,2,1,0:T(1,128)S(1)}, u32[]{:S(2)}, u32[]{:S(2)}) collective-permute-start(f32[6,1,6,1,128]{4,3,2,1,0:T(1,128)S(1)} %get-tuple-element.36), channel_id=1, source_target_pairs={{0,4},{1,5},{2,6},{3,7},{8,12},{9,13},{10,14},{11,15},{16,20},{17,... | collective-permute-start | bytes 55304 | tf_op jit(solution)/shard_map/ppermute | solution.py:16
  15.6 1.3 %collective-permute-start.3 = (f32[6,1,6,1,128]{4,3,2,1,0:T(1,128)S(1)}, f32[6,1,6,1,128]{4,3,2,1,0:T(1,128)S(1)}, u32[]{:S(2)}, u32[]{:S(2)}) collective-permute-start(f32[6,1,6,1,128]{4,3,2,1,0:T(1,128)S(1)} %get-tuple-element.37), channel_id=1, source_target_pairs={{4,0},{5,1},{6,2},{7,3},{12,8},{13,9},{14,10},{15,11},{20,16},{21,... | collective-permute-start | bytes 55304 | tf_op jit(solution)/shard_map/ppermute | solution.py:19
  17.0 4.2 %collective-permute-done.3 = f32[6,1,6,1,128]{4,3,2,1,0:T(1,128)S(1)} collective-permute-done((f32[6,1,6,1,128]{4,3,2,1,0:T(1,128)S(1)}, f32[6,1,6,1,128]{4,3,2,1,0:T(1,128)S(1)}, u32[]{:S(2)}, u32[]{:S(2)}) %collective-permute-start.3) | collective-permute-done | bytes 18464 | tf_op jit(solution)/shard_map/ppermute | solution.py:19
  21.5 1.3 %collective-permute-start.4 = (f32[6,1,6,10,1]{4,3,2,1,0:T(8,128)S(1)}, f32[6,1,6,10,1]{4,3,2,1,0:T(8,128)S(1)}, u32[]{:S(2)}, u32[]{:S(2)}) collective-permute-start(f32[6,1,6,10,1]{4,3,2,1,0:T(8,128)S(1)} %get-tuple-element.22), channel_id=1, source_target_pairs={{0,1},{1,2},{2,3},{4,5},{5,6},{6,7},{8,9},{9,10},{10,11},{12,13},{... | collective-permute-start | bytes 4328 | tf_op jit(solution)/shard_map/ppermute | solution.py:16
  23.0 1.9 %scatter_custom_fusion = f32[4096]{0:T(1024)S(1)} fusion(s32[256]{0:T(256)S(1)} %compare_select_fusion, f32[256]{0:T(256)S(1)} %bitcast.93, f32[]{:T(128)} %constant.92.clone.1), kind=kCustom, calls=%fused_computation.122 | custom fusion | flops 256 | bytes 16388 | tf_op jit(solution)/shard_map/scatter-add | solution.py:122
  25.0 1.3 %collective-permute-start.5 = (f32[6,1,6,10,1]{4,3,2,1,0:T(8,128)S(1)}, f32[6,1,6,10,1]{4,3,2,1,0:T(8,128)S(1)}, u32[]{:S(2)}, u32[]{:S(2)}) collective-permute-start(f32[6,1,6,10,1]{4,3,2,1,0:T(8,128)S(1)} %get-tuple-element.21), channel_id=1, source_target_pairs={{1,0},{2,1},{3,2},{5,4},{6,5},{7,6},{9,8},{10,9},{11,10},{13,12},{... | collective-permute-start | bytes 4328 | tf_op jit(solution)/shard_map/ppermute | solution.py:19
  26.3 0.4 maximum_maximum_fusion
  26.6 3.5 %collective-permute-done.5 = f32[6,1,6,10,1]{4,3,2,1,0:T(8,128)S(1)} collective-permute-done((f32[6,1,6,10,1]{4,3,2,1,0:T(8,128)S(1)}, f32[6,1,6,10,1]{4,3,2,1,0:T(8,128)S(1)}, u32[]{:S(2)}, u32[]{:S(2)}) %collective-permute-start.5) | collective-permute-done | bytes 1472 | tf_op jit(solution)/shard_map/ppermute | solution.py:19
  30.2 0.2 fusion.14
  30.7 3.5 %collective-permute-start.6 = (f32[6,1,1,8,128]{4,3,2,1,0:T(8,128)S(1)}, f32[6,1,1,8,128]{4,3,2,1,0:T(8,128)S(1)}, u32[]{:S(2)}, u32[]{:S(2)}) collective-permute-start(f32[6,1,1,8,128]{4,3,2,1,0:T(8,128)S(1)} %get-tuple-element.42), channel_id=1, source_target_pairs={{0,8},{8,16},{16,24},{1,9},{9,17},{17,25},{2,10},{10,18},{18,26},{... | collective-permute-start | bytes 73736 | tf_op jit(solution)/shard_map/ppermute | solution.py:16
  34.2 1.3 %collective-permute-start.7 = (f32[6,1,1,8,128]{4,3,2,1,0:T(8,128)S(1)}, f32[6,1,1,8,128]{4,3,2,1,0:T(8,128)S(1)}, u32[]{:S(2)}, u32[]{:S(2)}) collective-permute-start(f32[6,1,1,8,128]{4,3,2,1,0:T(8,128)S(1)} %get-tuple-element.43), channel_id=1, source_target_pairs={{8,0},{16,8},{24,16},{9,1},{17,9},{25,17},{10,2},{18,10},{26,18},{... | collective-permute-start | bytes 73736 | tf_op jit(solution)/shard_map/ppermute | solution.py:19
  35.5 0.2 collective-permute-done.6
  35.7 4.2 %collective-permute-done.7 = f32[6,1,1,8,128]{4,3,2,1,0:T(8,128)S(1)} collective-permute-done((f32[6,1,1,8,128]{4,3,2,1,0:T(8,128)S(1)}, f32[6,1,1,8,128]{4,3,2,1,0:T(8,128)S(1)}, u32[]{:S(2)}, u32[]{:S(2)}) %collective-permute-start.7) | collective-permute-done | bytes 24608 | tf_op jit(solution)/shard_map/ppermute | solution.py:19
  39.9 1.6 %collective-permute-start.8 = (f32[6,1,6,1,128]{4,3,2,1,0:T(1,128)S(1)}, f32[6,1,6,1,128]{4,3,2,1,0:T(1,128)S(1)}, u32[]{:S(2)}, u32[]{:S(2)}) collective-permute-start(f32[6,1,6,1,128]{4,3,2,1,0:T(1,128)S(1)} %get-tuple-element.34), channel_id=1, source_target_pairs={{0,4},{1,5},{2,6},{3,7},{8,12},{9,13},{10,14},{11,15},{16,20},{17,... | collective-permute-start | bytes 55304 | tf_op jit(solution)/shard_map/ppermute | solution.py:16
  41.6 1.3 %collective-permute-start.9 = (f32[6,1,6,1,128]{4,3,2,1,0:T(1,128)S(1)}, f32[6,1,6,1,128]{4,3,2,1,0:T(1,128)S(1)}, u32[]{:S(2)}, u32[]{:S(2)}) collective-permute-start(f32[6,1,6,1,128]{4,3,2,1,0:T(1,128)S(1)} %get-tuple-element.35), channel_id=1, source_target_pairs={{4,0},{5,1},{6,2},{7,3},{12,8},{13,9},{14,10},{15,11},{20,16},{21,... | collective-permute-start | bytes 55304 | tf_op jit(solution)/shard_map/ppermute | solution.py:19
  43.0 4.2 %collective-permute-done.9 = f32[6,1,6,1,128]{4,3,2,1,0:T(1,128)S(1)} collective-permute-done((f32[6,1,6,1,128]{4,3,2,1,0:T(1,128)S(1)}, f32[6,1,6,1,128]{4,3,2,1,0:T(1,128)S(1)}, u32[]{:S(2)}, u32[]{:S(2)}) %collective-permute-start.9) | collective-permute-done | bytes 18464 | tf_op jit(solution)/shard_map/ppermute | solution.py:19
  47.4 4.1 %collective-permute-start.10 = (f32[6,1,6,10,1]{4,3,2,1,0:T(8,128)S(1)}, f32[6,1,6,10,1]{4,3,2,1,0:T(8,128)S(1)}, u32[]{:S(2)}, u32[]{:S(2)}) collective-permute-start(f32[6,1,6,10,1]{4,3,2,1,0:T(8,128)S(1)} %get-tuple-element.20), channel_id=1, source_target_pairs={{0,1},{1,2},{2,3},{4,5},{5,6},{6,7},{8,9},{9,10},{10,11},{12,13},{... | collective-permute-start | bytes 4328 | tf_op jit(solution)/shard_map/ppermute | solution.py:16
  51.6 1.9 %scatter_custom_fusion.1 = f32[4096]{0:T(1024)S(1)} fusion(s32[256]{0:T(256)S(1)} %compare_select_fusion, f32[256]{0:T(256)S(1)} %bitcast.92, f32[]{:T(128)} %constant.92.clone.1), kind=kCustom, calls=%fused_computation.120 | custom fusion | flops 256 | bytes 16388 | tf_op jit(solution)/shard_map/scatter-add | solution.py:122
  53.5 1.3 %collective-permute-start.11 = (f32[6,1,6,10,1]{4,3,2,1,0:T(8,128)S(1)}, f32[6,1,6,10,1]{4,3,2,1,0:T(8,128)S(1)}, u32[]{:S(2)}, u32[]{:S(2)}) collective-permute-start(f32[6,1,6,10,1]{4,3,2,1,0:T(8,128)S(1)} %get-tuple-element.19), channel_id=1, source_target_pairs={{1,0},{2,1},{3,2},{5,4},{6,5},{7,6},{9,8},{10,9},{11,10},{13,12},{... | collective-permute-start | bytes 4328 | tf_op jit(solution)/shard_map/ppermute | solution.py:19
  54.8 0.4 maximum_maximum_fusion.1
  55.2 4.0 %collective-permute-done.11 = f32[6,1,6,10,1]{4,3,2,1,0:T(8,128)S(1)} collective-permute-done((f32[6,1,6,10,1]{4,3,2,1,0:T(8,128)S(1)}, f32[6,1,6,10,1]{4,3,2,1,0:T(8,128)S(1)}, u32[]{:S(2)}, u32[]{:S(2)}) %collective-permute-start.11) | collective-permute-done | bytes 1472 | tf_op jit(solution)/shard_map/ppermute | solution.py:19
  59.8 0.4 convolution_bitcast_fusion
  60.1 16.9 %psum.14 = f32[2,4]{1,0:T(2,128)S(1)} all-reduce(f32[2,4]{1,0:T(2,128)S(1)} %convolution_bitcast_fusion), channel_id=1, replica_groups=mesh['gx'=4,'gy'=2,'gz'=4] {'gy','gz'}, use_global_device_ids=true, to_apply=%region_3.4 | all-reduce | flops 8 | bytes 64 | tf_op jit(solution)/shard_map/psum | solution.py:144
  77.0 9.9 %psum.15 = f32[2,4]{1,0:T(2,128)S(1)} all-reduce(f32[2,4]{1,0:T(2,128)S(1)} %psum.14), channel_id=1, replica_groups=mesh['gx'=4,'gy'=2,'gz'=4] {'gx'}, use_global_device_ids=true, to_apply=%region_4.5 | all-reduce | flops 8 | bytes 64 | tf_op jit(solution)/shard_map/psum | solution.py:145
  86.9 0.3 fusion
  87.3 0.6 copy.56
  87.9 0.6 pad_maximum_fusion.11
  (52 shorter events, 2.1 us)
Async XLA Ops:
  0.6 59.1 %copy-start = (f32[4,4,8,128]{3,2,1,0:T(8,128)S(1)}, f32[4,4,8,128]{3,2,1,0:T(8,128)}, u32[]{:S(2)}) copy-start(f32[4,4,8,128]{3,2,1,0:T(8,128)} %param.13) | copy-start | bytes 196612
  0.6 7.1 %copy-start.2 = (bf16[2,3,1,4,8,128]{5,4,3,2,1,0:T(8,128)(2,1)S(1)}, bf16[2,3,1,4,8,128]{5,4,3,2,1,0:T(8,128)(2,1)}, u32[]{:S(2)}) copy-start(bf16[2,3,1,4,8,128]{5,4,3,2,1,0:T(8,128)(2,1)} %param.8) | copy-start | bytes 147460
  1.5 7.1 %collective-permute-start = (f32[6,1,1,8,128]{4,3,2,1,0:T(8,128)S(1)}, f32[6,1,1,8,128]{4,3,2,1,0:T(8,128)S(1)}, u32[]{:S(2)}, u32[]{:S(2)}) collective-permute-start(f32[6,1,1,8,128]{4,3,2,1,0:T(8,128)S(1)} %get-tuple-element.45), channel_id=1, source_target_pairs={{0,8},{8,16},{16,24},{1,9},{9,17},{17,25},{2,10},{10,18},{18,26},{... | collective-permute-start | bytes 73736 | tf_op jit(solution)/shard_map/ppermute | solution.py:16
  6.4 5.7 %collective-permute-start.1 = (f32[6,1,1,8,128]{4,3,2,1,0:T(8,128)S(1)}, f32[6,1,1,8,128]{4,3,2,1,0:T(8,128)S(1)}, u32[]{:S(2)}, u32[]{:S(2)}) collective-permute-start(f32[6,1,1,8,128]{4,3,2,1,0:T(8,128)S(1)} %get-tuple-element.44), channel_id=1, source_target_pairs={{8,0},{16,8},{24,16},{9,1},{17,9},{25,17},{10,2},{18,10},{26,18},{... | collective-permute-start | bytes 73736 | tf_op jit(solution)/shard_map/ppermute | solution.py:19
  7.7 0.9 %copy-start.1 = (f32[6,1,4,8,128]{4,3,2,1,0:T(8,128)S(1)}, f32[6,1,4,8,128]{4,3,2,1,0:T(8,128)}, u32[]{:S(2)}) copy-start(f32[6,1,4,8,128]{4,3,2,1,0:T(8,128)} %param.7) | copy-start | bytes 294916
  7.9 0.7 copy-start.4
  12.1 4.7 %copy-start.5 = (s32[256]{0:T(256)S(1)}, s32[256]{0:T(256)}, u32[]{:S(2)}) copy-start(s32[256]{0:T(256)} %param.11) | copy-start | bytes 3076
  12.1 4.9 %collective-permute-start.2 = (f32[6,1,6,1,128]{4,3,2,1,0:T(1,128)S(1)}, f32[6,1,6,1,128]{4,3,2,1,0:T(1,128)S(1)}, u32[]{:S(2)}, u32[]{:S(2)}) collective-permute-start(f32[6,1,6,1,128]{4,3,2,1,0:T(1,128)S(1)} %get-tuple-element.36), channel_id=1, source_target_pairs={{0,4},{1,5},{2,6},{3,7},{8,12},{9,13},{10,14},{11,15},{16,20},{17,... | collective-permute-start | bytes 55304 | tf_op jit(solution)/shard_map/ppermute | solution.py:16
  15.6 5.7 %collective-permute-start.3 = (f32[6,1,6,1,128]{4,3,2,1,0:T(1,128)S(1)}, f32[6,1,6,1,128]{4,3,2,1,0:T(1,128)S(1)}, u32[]{:S(2)}, u32[]{:S(2)}) collective-permute-start(f32[6,1,6,1,128]{4,3,2,1,0:T(1,128)S(1)} %get-tuple-element.37), channel_id=1, source_target_pairs={{4,0},{5,1},{6,2},{7,3},{12,8},{13,9},{14,10},{15,11},{20,16},{21,... | collective-permute-start | bytes 55304 | tf_op jit(solution)/shard_map/ppermute | solution.py:19
  21.3 1.5 %copy-start.3 = (s32[4,8,128]{2,1,0:T(8,128)S(1)}, s32[4,8,128]{2,1,0:T(8,128)}, u32[]{:S(2)}) copy-start(s32[4,8,128]{2,1,0:T(8,128)} %param.9) | copy-start | bytes 49156
  21.5 1.3 %copy-start.6 = (s32[32]{0:T(128)S(1)}, s32[32]{0:T(128)}, u32[]{:S(2)}) copy-start(s32[32]{0:T(128)} %param.10) | copy-start | bytes 388
  21.5 4.8 %collective-permute-start.4 = (f32[6,1,6,10,1]{4,3,2,1,0:T(8,128)S(1)}, f32[6,1,6,10,1]{4,3,2,1,0:T(8,128)S(1)}, u32[]{:S(2)}, u32[]{:S(2)}) collective-permute-start(f32[6,1,6,10,1]{4,3,2,1,0:T(8,128)S(1)} %get-tuple-element.22), channel_id=1, source_target_pairs={{0,1},{1,2},{2,3},{4,5},{5,6},{6,7},{8,9},{9,10},{10,11},{12,13},{... | collective-permute-start | bytes 4328 | tf_op jit(solution)/shard_map/ppermute | solution.py:16
  25.0 5.2 %collective-permute-start.5 = (f32[6,1,6,10,1]{4,3,2,1,0:T(8,128)S(1)}, f32[6,1,6,10,1]{4,3,2,1,0:T(8,128)S(1)}, u32[]{:S(2)}, u32[]{:S(2)}) collective-permute-start(f32[6,1,6,10,1]{4,3,2,1,0:T(8,128)S(1)} %get-tuple-element.21), channel_id=1, source_target_pairs={{1,0},{2,1},{3,2},{5,4},{6,5},{7,6},{9,8},{10,9},{11,10},{13,12},{... | collective-permute-start | bytes 4328 | tf_op jit(solution)/shard_map/ppermute | solution.py:19
  30.7 5.0 %collective-permute-start.6 = (f32[6,1,1,8,128]{4,3,2,1,0:T(8,128)S(1)}, f32[6,1,1,8,128]{4,3,2,1,0:T(8,128)S(1)}, u32[]{:S(2)}, u32[]{:S(2)}) collective-permute-start(f32[6,1,1,8,128]{4,3,2,1,0:T(8,128)S(1)} %get-tuple-element.42), channel_id=1, source_target_pairs={{0,8},{8,16},{16,24},{1,9},{9,17},{17,25},{2,10},{10,18},{18,26},{... | collective-permute-start | bytes 73736 | tf_op jit(solution)/shard_map/ppermute | solution.py:16
  34.2 5.7 %collective-permute-start.7 = (f32[6,1,1,8,128]{4,3,2,1,0:T(8,128)S(1)}, f32[6,1,1,8,128]{4,3,2,1,0:T(8,128)S(1)}, u32[]{:S(2)}, u32[]{:S(2)}) collective-permute-start(f32[6,1,1,8,128]{4,3,2,1,0:T(8,128)S(1)} %get-tuple-element.43), channel_id=1, source_target_pairs={{8,0},{16,8},{24,16},{9,1},{17,9},{25,17},{10,2},{18,10},{26,18},{... | collective-permute-start | bytes 73736 | tf_op jit(solution)/shard_map/ppermute | solution.py:19
  39.9 3.1 %collective-permute-start.8 = (f32[6,1,6,1,128]{4,3,2,1,0:T(1,128)S(1)}, f32[6,1,6,1,128]{4,3,2,1,0:T(1,128)S(1)}, u32[]{:S(2)}, u32[]{:S(2)}) collective-permute-start(f32[6,1,6,1,128]{4,3,2,1,0:T(1,128)S(1)} %get-tuple-element.34), channel_id=1, source_target_pairs={{0,4},{1,5},{2,6},{3,7},{8,12},{9,13},{10,14},{11,15},{16,20},{17,... | collective-permute-start | bytes 55304 | tf_op jit(solution)/shard_map/ppermute | solution.py:16
  41.6 5.7 %collective-permute-start.9 = (f32[6,1,6,1,128]{4,3,2,1,0:T(1,128)S(1)}, f32[6,1,6,1,128]{4,3,2,1,0:T(1,128)S(1)}, u32[]{:S(2)}, u32[]{:S(2)}) collective-permute-start(f32[6,1,6,1,128]{4,3,2,1,0:T(1,128)S(1)} %get-tuple-element.35), channel_id=1, source_target_pairs={{4,0},{5,1},{6,2},{7,3},{12,8},{13,9},{14,10},{15,11},{20,16},{21,... | collective-permute-start | bytes 55304 | tf_op jit(solution)/shard_map/ppermute | solution.py:19
  47.4 7.4 %collective-permute-start.10 = (f32[6,1,6,10,1]{4,3,2,1,0:T(8,128)S(1)}, f32[6,1,6,10,1]{4,3,2,1,0:T(8,128)S(1)}, u32[]{:S(2)}, u32[]{:S(2)}) collective-permute-start(f32[6,1,6,10,1]{4,3,2,1,0:T(8,128)S(1)} %get-tuple-element.20), channel_id=1, source_target_pairs={{0,1},{1,2},{2,3},{4,5},{5,6},{6,7},{8,9},{9,10},{10,11},{12,13},{... | collective-permute-start | bytes 4328 | tf_op jit(solution)/shard_map/ppermute | solution.py:16
  53.5 5.7 %collective-permute-start.11 = (f32[6,1,6,10,1]{4,3,2,1,0:T(8,128)S(1)}, f32[6,1,6,10,1]{4,3,2,1,0:T(8,128)S(1)}, u32[]{:S(2)}, u32[]{:S(2)}) collective-permute-start(f32[6,1,6,10,1]{4,3,2,1,0:T(8,128)S(1)} %get-tuple-element.19), channel_id=1, source_target_pairs={{1,0},{2,1},{3,2},{5,4},{6,5},{7,6},{9,8},{10,9},{11,10},{13,12},{... | collective-permute-start | bytes 4328 | tf_op jit(solution)/shard_map/ppermute | solution.py:19
